TPU v7x, 256 devices: a whole 4x4x8 slice. The times are simulated.
256 devices in a mesh: seq: 16 (over y, x_hi, core), ch: 16 (over z, x_lo).
Axes of the slice: x: 4 (x_hi: 2, x_lo: 2; x = x_hi * 2 + x_lo), y: 4, z: 8, core: 2. Of those that a mesh axis runs over, the one named last changes fastest.
Arguments:
- tokens: bfloat16 [8192, 4096], P('seq'), may hold values from -6 to 6
- in_weight: bfloat16 [4096, 3, 4096], P(None, None, 'ch'), may hold values from -0.09375 to 0.09375
- short_taps: float32 [3, 3, 4096], P(None, None, 'ch'), may hold values from -3 to 3
- band_freq: float32 [16], replicated, may hold values from 1 to 512
- filter_first: float32 [33, 64], replicated, may hold values from -6 to 6
- filter_bias: float32 [64], replicated, may hold values from -3.140625 to 3.140625
- filter_out: float32 [64, 4096], P(None, 'ch'), may hold values from -0.0234375 to 0.0234375
- decay: float32 [4096], P('ch'), may hold values from 1.2207031e-05 to 0.02
- out_weight: bfloat16 [4096, 4096], P('ch'), may hold values from -0.125 to 0.125
Outputs:
- layer_out: bfloat16 [8192, 4096], P('seq', 'ch')
All inputs are finite; a program needn't handle non-finite values.
Results may differ from a plain program's by a relative error of at most 0.03.
Values may be sent and summed in bfloat16 or wider, within the bound.
A program may use at most 128 MiB of HBM per device.

v0:
```python
import functools
import math

import jax
import jax.numpy as jnp
import numpy as np
from jax import lax
from jax.experimental import pallas as pl
from jax.experimental.pallas import tpu as pltpu
from jax.sharding import PartitionSpec as P

MESH = pl.DeviceIdType.MESH
BF = jnp.bfloat16
F32 = jnp.float32
HIGH = lax.Precision.HIGHEST
RADIX = 128
HALF = 80


def dft_tables(rows_in):
    full = RADIX * RADIX
    k1 = np.arange(HALF)[:, None]
    used = (k1 <= RADIX // 2).astype(np.float64)
    line = np.arange(RADIX)
    a = 2 * np.pi * k1 * np.arange(rows_in)[None, :] / RADIX
    outer = np.concatenate([np.cos(a) * used, -np.sin(a) * used], 0)
    tw = 2 * np.pi * k1 * line[None, :] / full
    twist = np.stack([np.cos(tw), np.sin(tw)])
    b = 2 * np.pi * np.outer(line, line) / RADIX
    co, si = np.cos(b), np.sin(b)
    inner = np.block([[co, -si], [si, co]])
    inner_back = np.block([[co, si], [-si, co]])
    weight = np.where((k1 == 0) | (k1 == RADIX // 2), 1.0, 2.0) * used / full
    outer_back = np.concatenate([(np.cos(a) * weight).T, (-np.sin(a) * weight).T], 1)
    return (
        jnp.asarray(outer, BF),
        jnp.asarray(twist, F32),
        jnp.asarray(inner, BF),
        jnp.asarray(inner_back, BF),
        jnp.asarray(outer_back, BF),
    )


def sin_turns(turns):
    turns = turns - 0.25
    turns = turns - jnp.round(turns)
    x = (0.25 - jnp.abs(turns)) * (2.0 * math.pi)
    x2 = x * x
    p = jnp.float32(-2.50521083854e-8)
    for c in (2.75573192239858e-6, -1.98412698412698e-4, 8.33333333333333e-3, -1.66666666666667e-1):
        p = p * x2 + jnp.float32(c)
    return x + x * x2 * p


def first_row(v):
    row = lax.broadcasted_iota(jnp.int32, (8, v.shape[1]), 0)
    return jnp.where(row == 0, jnp.broadcast_to(v, (8, v.shape[1])), 0.0)


def contract_rows(a, b):
    return lax.dot_general(a, b, (((0,), (0,)), ((), ())), precision=HIGH, preferred_element_type=F32)


def outer_product(v, w):
    return contract_rows(first_row(v), first_row(w))


def forward(grid32, x_all, a_all, rows_all, outer, twist, inner, spec_ref, channels):
    rows_in = x_all.shape[0]
    for c in range(channels):
        x_all[:, c * RADIX : (c + 1) * RADIX] = grid32[pl.ds(c, rows_in, stride=channels), :].astype(BF)
    a_all[...] = jnp.dot(outer[...], x_all[...], preferred_element_type=F32)
    co, si = twist[0], twist[1]
    for c in range(channels):
        lanes = slice(c * RADIX, (c + 1) * RADIX)
        re, im = a_all[:HALF, lanes], a_all[HALF:, lanes]
        rows = slice(c * HALF, (c + 1) * HALF)
        rows_all[rows, :RADIX] = (re * co + im * si).astype(BF)
        rows_all[rows, RADIX:] = (im * co - re * si).astype(BF)
    spec_ref[...] = jnp.dot(rows_all[...], inner[...], preferred_element_type=F32)


def operator_kernel(
    n_seq,
    tok_hbm, w_hbm, taps, band, first, bias, fout, decay, outer_hbm, twist_hbm, inner_hbm, inner_back_hbm, outer_back_hbm,
    gated_ref,
    tok, w, outer, twist, inner, inner_back, outer_back,
    px, gate, halo_s, halo_r, send4, imp4, imp_recv, src_recv, conv_send, conv4,
    grid32, x_all, a_all, rows_all, imp_spec, src_spec,
    load_sem, halo_sem, imp_ssem, imp_rsem, src_ssem, src_rsem, conv_ssem, conv_rsem, own_sem,
):
    me = lax.axis_index("seq")
    rows, width = tok_hbm.shape
    slab = w_hbm.shape[2]
    channels = slab // n_seq
    per = rows // RADIX
    half = rows // 2
    length = rows * n_seq

    loads = [
        pltpu.make_async_copy(w_hbm.at[0], w.at[0], load_sem.at[0]),
        pltpu.make_async_copy(w_hbm.at[2], w.at[2], load_sem.at[1]),
        pltpu.make_async_copy(tok_hbm.at[half:], tok.at[half:], load_sem.at[2]),
        pltpu.make_async_copy(tok_hbm.at[:half], tok.at[:half], load_sem.at[3]),
        pltpu.make_async_copy(w_hbm.at[1], w.at[1], load_sem.at[4]),
        pltpu.make_async_copy(outer_hbm, outer, load_sem.at[5]),
        pltpu.make_async_copy(twist_hbm, twist, load_sem.at[6]),
        pltpu.make_async_copy(inner_hbm, inner, load_sem.at[7]),
        pltpu.make_async_copy(inner_back_hbm, inner_back, load_sem.at[8]),
        pltpu.make_async_copy(outer_back_hbm, outer_back, load_sem.at[9]),
    ]
    for copy in loads:
        copy.start()

    barrier = pltpu.get_barrier_semaphore()

    def greet(d, carry):
        pl.semaphore_signal(barrier, inc=1, device_id={"seq": lax.rem(me + d, n_seq)}, device_id_type=MESH)
        return carry

    lax.fori_loop(1, n_seq, greet, 0)

    pos = (me * rows + lax.broadcasted_iota(jnp.int32, (1, rows), 1)).astype(F32)
    scaled = pos * (1.0 / length)
    turns = outer_product(band[...], scaled)
    turns = turns - jnp.round(turns)
    n_band = band.shape[1]
    head = lax.broadcasted_iota(jnp.int32, (8, rows), 0)
    features = jnp.concatenate(
        [sin_turns(turns + 0.25), sin_turns(turns), jnp.where(head == 0, scaled, jnp.where(head == 1, 1.0, 0.0))], 0
    )
    head = lax.broadcasted_iota(jnp.int32, (8, first.shape[1]), 0)
    layer = jnp.concatenate(
        [
            first[1 : 1 + n_band, :],
            first[1 + n_band :, :],
            jnp.where(head == 0, first[0:1, :], jnp.where(head == 1, bias[...], 0.0)),
        ],
        0,
    )
    pre = contract_rows(layer, features)
    hidden = sin_turns(pre * (1.0 / (2.0 * math.pi)))
    impulse = contract_rows(fout[...], hidden) * jnp.exp(-outer_product(decay[...], pos))
    for q in range(per):
        imp4[q] = impulse[:, q * RADIX : (q + 1) * RADIX].astype(BF)

    pl.semaphore_wait(barrier, n_seq - 1)

    def spread_copy(src, dst, ssem, rsem, peer):
        return pltpu.make_async_remote_copy(
            src_ref=src.at[:, pl.ds(pl.multiple_of(peer * channels, channels), channels), :],
            dst_ref=dst.at[pl.ds(me * per, per)],
            send_sem=ssem.at[peer],
            recv_sem=rsem.at[me],
            device_id={"seq": peer},
            device_id_type=MESH,
        )

    def arrive(dst, ssem, rsem, peer):
        return pltpu.make_async_remote_copy(
            src_ref=dst.at[pl.ds(peer * per, per)],
            dst_ref=dst.at[pl.ds(peer * per, per)],
            send_sem=ssem.at[peer],
            recv_sem=rsem.at[peer],
            device_id={"seq": peer},
            device_id_type=MESH,
        )

    def own_piece(src, dst):
        dst[pl.ds(me * per, per)] = src[:, pl.ds(pl.multiple_of(me * channels, channels), channels), :]

    def each_peer(step):
        def body(d, carry):
            step(lax.rem(me + d, n_seq))
            return carry

        lax.fori_loop(1, n_seq, body, 0)

    each_peer(lambda p: spread_copy(imp4, imp_recv, imp_ssem, imp_rsem, p).start())
    own_piece(imp4, imp_recv)

    after = lax.rem(me + 1, n_seq)
    before = lax.rem(me + n_seq - 1, n_seq)

    def halo_copy(g):
        return pltpu.make_async_remote_copy(
            src_ref=halo_s.at[g], dst_ref=halo_r.at[g], send_sem=halo_sem.at[0, g], recv_sem=halo_sem.at[1, g],
            device_id={"seq": after}, device_id_type=MESH,
        )

    def project(g, part):
        out = jnp.dot(tok[part * half : (part + 1) * half, :], w[g], preferred_element_type=F32).astype(BF)
        px[g, 16 + part * half : 16 + (part + 1) * half, :] = out.astype(F32)
        if part == 1:
            halo_s[g] = out[half - 16 :, :]
            halo_copy(g).start()

    def take_halo(g):
        halo_copy(g).wait()
        px[g, 0:16, :] = jnp.where(me > 0, halo_r[g].astype(F32), 0.0)

    def mixed(g, q):
        total = taps[0, g : g + 1, :] * px[g, 16 + q * RADIX : 16 + (q + 1) * RADIX, :]
        for i in (1, 2):
            total = total + taps[i, g : g + 1, :] * px[g, 16 - i + q * RADIX : 16 - i + (q + 1) * RADIX, :]
        return total

    loads[0].wait()
    loads[1].wait()
    loads[2].wait()
    project(0, 1)
    project(2, 1)
    loads[3].wait()
    project(0, 0)
    project(2, 0)
    take_halo(0)
    take_halo(2)
    for q in range(per):
        send4[q] = (mixed(0, q) * mixed(2, q)).T.astype(BF)
    each_peer(lambda p: spread_copy(send4, src_recv, src_ssem, src_rsem, p).start())
    own_piece(send4, src_recv)

    loads[4].wait()
    project(1, 1)
    project(1, 0)
    take_halo(1)
    for q in range(per):
        gate[q * RADIX : (q + 1) * RADIX, :] = mixed(1, q)

    for copy in loads[5:]:
        copy.wait()
    each_peer(lambda p: arrive(imp_recv, imp_ssem, imp_rsem, p).wait_recv())
    points = per * n_seq
    grid32[...] = imp_recv[...].astype(F32).reshape(points * channels, RADIX)
    forward(grid32, x_all, a_all, rows_all, outer, twist, inner, imp_spec, channels)

    each_peer(lambda p: arrive(src_recv, src_ssem, src_rsem, p).wait_recv())
    grid32[...] = src_recv[...].astype(F32).reshape(points * channels, RADIX)
    forward(grid32, x_all, a_all, rows_all, outer, twist, inner, src_spec, channels)

    for c in range(channels):
        line = slice(c * HALF, (c + 1) * HALF)
        sre, sim = src_spec[line, :RADIX], src_spec[line, RADIX:]
        ire, iim = imp_spec[line, :RADIX], imp_spec[line, RADIX:]
        rows_all[line, :RADIX] = (sre * ire - sim * iim).astype(BF)
        rows_all[line, RADIX:] = (sre * iim + sim * ire).astype(BF)
    src_spec[...] = jnp.dot(rows_all[...], inner_back[...], preferred_element_type=F32)
    co, si = twist[0], twist[1]
    for c in range(channels):
        line = slice(c * HALF, (c + 1) * HALF)
        lanes = slice(c * RADIX, (c + 1) * RADIX)
        re, im = src_spec[line, :RADIX], src_spec[line, RADIX:]
        back = jnp.concatenate([re * co - im * si, im * co + re * si], 0).astype(BF)
        y = jnp.dot(outer_back[...], back, preferred_element_type=F32)
        grid32[pl.ds(c, points, stride=channels), :] = y
    conv_send[...] = grid32[...].astype(BF).reshape(points, channels, RADIX)

    def return_copy(peer):
        return pltpu.make_async_remote_copy(
            src_ref=conv_send.at[pl.ds(peer * per, per)],
            dst_ref=conv4.at[:, pl.ds(pl.multiple_of(me * channels, channels), channels), :],
            send_sem=conv_ssem.at[peer],
            recv_sem=conv_rsem.at[me],
            device_id={"seq": peer},
            device_id_type=MESH,
        )

    def return_arrive(peer):
        piece = conv4.at[:, pl.ds(pl.multiple_of(peer * channels, channels), channels), :]
        return pltpu.make_async_remote_copy(
            src_ref=piece, dst_ref=piece, send_sem=conv_ssem.at[peer], recv_sem=conv_rsem.at[peer],
            device_id={"seq": peer}, device_id_type=MESH,
        )

    each_peer(lambda p: return_copy(p).start())
    conv4[:, pl.ds(pl.multiple_of(me * channels, channels), channels), :] = conv_send[pl.ds(me * per, per)]
    each_peer(lambda p: return_arrive(p).wait_recv())
    for q in range(per):
        line = slice(q * RADIX, (q + 1) * RADIX)
        gated_ref[line, :] = (gate[line, :] * conv4[q].astype(F32).T).astype(BF)

    each_peer(lambda p: spread_copy(imp4, imp_recv, imp_ssem, imp_rsem, p).wait_send())
    each_peer(lambda p: spread_copy(send4, src_recv, src_ssem, src_rsem, p).wait_send())
    each_peer(lambda p: return_copy(p).wait_send())


def gated_rows(n_seq, tokens, in_weight, short_taps, band_freq, filter_first, filter_bias, filter_out, decay):
    rows, width = tokens.shape
    slab = in_weight.shape[2]
    channels = slab // n_seq
    per = rows // RADIX
    points = per * n_seq
    tables = dft_tables(points)
    anyspec = pl.BlockSpec(memory_space=pl.ANY)
    vspec = pl.BlockSpec(memory_space=pltpu.VMEM)
    dma = pltpu.SemaphoreType.DMA
    scratch = [
        pltpu.VMEM((rows, width), BF),
        pltpu.VMEM((3, width, slab), BF),
        *[pltpu.VMEM(t.shape, t.dtype) for t in tables],
        pltpu.VMEM((3, rows + 16, slab), F32),
        pltpu.VMEM((rows, slab), F32),
        pltpu.VMEM((3, 16, slab), BF),
        pltpu.VMEM((3, 16, slab), BF),
        pltpu.VMEM((per, slab, RADIX), BF),
        pltpu.VMEM((per, slab, RADIX), BF),
        pltpu.VMEM((points, channels, RADIX), BF),
        pltpu.VMEM((points, channels, RADIX), BF),
        pltpu.VMEM((points, channels, RADIX), BF),
        pltpu.VMEM((per, slab, RADIX), BF),
        pltpu.VMEM((points * channels, RADIX), F32),
        pltpu.VMEM((points, channels * RADIX), BF),
        pltpu.VMEM((2 * HALF, channels * RADIX), F32),
        pltpu.VMEM((channels * HALF, 2 * RADIX), BF),
        pltpu.VMEM((channels * HALF, 2 * RADIX), F32),
        pltpu.VMEM((channels * HALF, 2 * RADIX), F32),
        dma((10,)), dma((2, 3)), dma((n_seq,)), dma((n_seq,)), dma((n_seq,)), dma((n_seq,)), dma((n_seq,)), dma((n_seq,)), dma,
    ]
    return pl.pallas_call(
        functools.partial(operator_kernel, n_seq),
        out_shape=jax.ShapeDtypeStruct((rows, slab), BF),
        in_specs=[anyspec] * 2 + [vspec] * 6 + [anyspec] * 5,
        out_specs=vspec,
        scratch_shapes=scratch,
        compiler_params=pltpu.CompilerParams(collective_id=0, has_side_effects=True, vmem_limit_bytes=56 * 2**20),
        cost_estimate=pl.CostEstimate(flops=2 * rows * width * slab * 3, bytes_accessed=12 * 2**20, transcendentals=0),
    )(
        tokens, jnp.transpose(in_weight, (1, 0, 2)), short_taps, band_freq[None, :], filter_first, filter_bias[None, :],
        filter_out, decay[None, :], *tables,
    )


def local(tokens, in_weight, short_taps, band_freq, filter_first, filter_bias, filter_out, decay, out_weight):
    gated_out = gated_rows(
        lax.axis_size("seq"), tokens, in_weight, short_taps, band_freq, filter_first, filter_bias, filter_out, decay
    )
    summed = lax.psum_scatter(
        lax.dot_general(
            out_weight, gated_out, (((0,), (1,)), ((), ())), preferred_element_type=jnp.float32
        ).astype(jnp.bfloat16),
        "ch",
        scatter_dimension=0,
        tiled=True,
    ).astype(jnp.float32)
    return summed.T.astype(jnp.bfloat16)


def solution(mesh):
    in_specs = (
        P("seq", None),
        P(None, None, "ch"),
        P(None, None, "ch"),
        P(),
        P(),
        P(),
        P(None, "ch"),
        P("ch"),
        P("ch", None),
    )
    out_specs = P("seq", "ch")
    return jax.shard_map(local, mesh=mesh, in_specs=in_specs, out_specs=out_specs, check_vma=False)
```

profile of v0, /device:TPU:1, one launch (start us, length us, event | category | flops | bytes accessed | tf_op | source)
XLA Modules:
  0.0 144.5 jit_solution(1618667923413460272)
XLA Ops:
  6.5 0.0 copy-start
  6.5 0.0 reduce-scatter.2.cloned.1.call-start
  6.5 28.6 %shard_map.136 = bf16[512,256]{1,0:T(8,128)(2,1)} custom-call(bf16[512,4096]{1,0:T(8,128)(2,1)} %tok_hbm.1, bf16[3,4096,256]{2,1,0:T(8,128)(2,1)} %bitcast.9, f32[3,3,256]{2,1,0:T(4,128)} %taps.1, f32[1,16]{1,0:T(1,128)} %bitcast.11, f32[33,64]{1,0:T(8,128)} %first.1, f32[1,64]{1,0:T(1,128)} %bitcast.12, f32[64,256]{1,0:T(8,128)} %fout.1, ...), custom_call_target="tpu_custom_call" | custom-call | flops 3221225472 | bytes 12582912 | tf_op jit(solution)/shard_map/pallas_call | solution.py:319
  35.2 0.0 copy-done
  35.2 4.1 %fusion = bf16[4096,512]{0,1:T(8,128)(2,1)} fusion(bf16[512,256]{1,0:T(8,128)(2,1)} %shard_map.136, bf16[256,4096]{1,0:T(8,128)(2,1)S(1)} %copy-done), kind=kOutput, calls=%fused_computation.1 | convolution fusion | flops 1075838976 | bytes 6553600 | tf_op jit(solution)/shard_map/dot_general | solution.py:338
  39.3 0.0 reduce-scatter.2.cloned.1.call-update
  39.4 98.3 %reduce-scatter.2.cloned.1.call-done = bf16[256,512]{0,1:T(8,128)(2,1)} async-done(((bf16[4096,512]{0,1:T(8,128)(2,1)}), bf16[256,512]{0,1:T(8,128)(2,1)}) %reduce-scatter.2.cloned.1.call-update) | async-done | bytes 262160 | tf_op jit(solution)/shard_map/reduce_scatter | solution.py:337
Async XLA Ops:
  6.5 28.7 %copy-start = (bf16[256,4096]{1,0:T(8,128)(2,1)S(1)}, bf16[256,4096]{1,0:T(8,128)(2,1)}, u32[]{:S(2)}) copy-start(bf16[256,4096]{1,0:T(8,128)(2,1)} %param.22) | copy-start | bytes 6291460
  6.5 131.1 %reduce-scatter.2.cloned.1.call-start = ((), (), s32[]{:S(2)}) async-start(), calls=%async_computation.1 | async-start | bytes 4456448 | tf_op jit(solution)/shard_map/reduce_scatter | solution.py:337
Sparse Core Ops, SparseCore 0:
  39.5 98.0 reduce-scatter.1
where the time goes:
time: 146 us; the launch traced here: 144 us
  waiting for transfers between devices  98.3 us (67%)
  Pallas kernels  28.6 us (20%)
  between operations  13.4 us (9%)
  matrix products  4.15 us (3%)
    reduce_scatter x1, waiting for transfers between devices, local(): lax.psum_scatter(lax.dot_general(out_weight, gated_out, (((0,), (1,)), ((...  98.3 us
    pallas_call x1, Pallas kernels, gated_rows(): pl.pallas_call(functools.partial(operator_kernel, n_seq), out_shape=jax.S...  28.6 us
    dot_general x1, matrix products, local(): lax.dot_general(out_weight, gated_out, (((0,), (1,)), ((), ())), preferre...  4.15 us
  transfers between devices with their start and end apart: 1, of which 1 were waited for; matrix products, arithmetic and copies ran while one was open for 0% of the time, Pallas kernels for 0%

commit v1 on v0

--- a/solution.py
+++ b/solution.py
@@ -80,16 +80,189 @@
     spec_ref[...] = jnp.dot(rows_all[...], inner[...], preferred_element_type=F32)
 
 
+CHUNK = 64
+
+
+class Spread:
+    def __init__(self, n_ch, w_hbm, out_ref, wout, g2, sums, landed, wl_sem, wx_ssem, wx_rsem, wc_sem, gx_ssem, gx_rsem, r_ssem, r_rsem):
+        self.__dict__.update(locals())
+        del self.__dict__["self"]
+        self.n_z = n_ch // 2
+        self.c = lax.axis_index("ch")
+        self.z = self.c // 2
+        self.xl = lax.rem(self.c, 2)
+        self.s = lax.axis_index("seq")
+        self.core = lax.rem(self.s, 2)
+        self.partner = {"ch": self.c + 1 - 2 * self.xl}
+        self.sibling = {"seq": self.s + 1 - 2 * self.core}
+        self.up = {"ch": lax.rem(self.c + 2, n_ch)}
+        self.down = {"ch": lax.rem(self.c + n_ch - 2, n_ch)}
+        self.depth = w_hbm.shape[0]
+        self.cols = w_hbm.shape[1] // n_ch
+        self.rows = out_ref.shape[0]
+        self.chunks = self.rows // CHUNK
+
+    def peers(self):
+        return [self.partner, self.up, self.down]
+
+    def _columns(self, block):
+        return pl.ds(pl.multiple_of(block * self.cols, self.cols), self.cols)
+
+    def own_weight(self, j):
+        return pltpu.make_async_copy(
+            self.w_hbm.at[:, self._columns(2 * j + self.xl)], self.wout.at[0, j], self.wl_sem.at[j]
+        )
+
+    def weight_to_partner(self, j):
+        half = self.depth // 2
+        part = pl.ds(pl.multiple_of(self.core * half, half), half)
+        return pltpu.make_async_remote_copy(
+            src_ref=self.w_hbm.at[part, self._columns(2 * j + 1 - self.xl)],
+            dst_ref=self.wout.at[1, j, part, :],
+            send_sem=self.wx_ssem.at[j], recv_sem=self.wx_rsem.at[j], device_id=self.partner, device_id_type=MESH,
+        )
+
+    def weight_to_sibling(self):
+        half = self.depth // 2
+        part = pl.ds(pl.multiple_of(self.core * half, half), half)
+        return pltpu.make_async_remote_copy(
+            src_ref=self.wout.at[1, :, part, :], dst_ref=self.wout.at[1, :, part, :],
+            send_sem=self.wc_sem.at[0], recv_sem=self.wc_sem.at[1], device_id=self.sibling, device_id_type=MESH,
+        )
+
+    def weight_from_sibling(self):
+        half = self.depth // 2
+        part = pl.ds(pl.multiple_of((1 - self.core) * half, half), half)
+        return pltpu.make_async_remote_copy(
+            src_ref=self.wout.at[1, :, part, :], dst_ref=self.wout.at[1, :, part, :],
+            send_sem=self.wc_sem.at[0], recv_sem=self.wc_sem.at[1], device_id=self.sibling, device_id_type=MESH,
+        )
+
+    def start_weights(self):
+        for j in range(self.n_z):
+            self.weight_to_partner(j).start()
+
+    def load_weights(self):
+        for j in range(self.n_z):
+            self.own_weight(j).start()
+
+    def pass_weights(self):
+        for j in range(self.n_z):
+            self.weight_to_partner(j).wait()
+        self.weight_to_sibling().start()
+
+    def gated_to_partner(self, q):
+        line = slice(q * RADIX, (q + 1) * RADIX)
+        return pltpu.make_async_remote_copy(
+            src_ref=self.g2.at[0, line], dst_ref=self.g2.at[1, line],
+            send_sem=self.gx_ssem.at[q], recv_sem=self.gx_rsem.at[q], device_id=self.partner, device_id_type=MESH,
+        )
+
+    def hop(self, way, step, i):
+        return pltpu.make_async_remote_copy(
+            src_ref=self.sums.at[way, step, i], dst_ref=self.landed.at[way, step, i],
+            send_sem=self.r_ssem.at[way, step, i], recv_sem=self.r_rsem.at[way, step, i],
+            device_id=(self.up, self.down)[way], device_id_type=MESH,
+        )
+
+    def partial_sum(self, block, i):
+        line = pl.ds(pl.multiple_of(i * CHUNK, CHUNK), CHUNK)
+        return jnp.dot(self.g2[0, line], self.wout[0, block], preferred_element_type=F32) + jnp.dot(
+            self.g2[1, line], self.wout[1, block], preferred_element_type=F32
+        )
+
+    def block_at(self, way, step):
+        n = self.n_z
+        if way == 0:
+            return lax.rem(self.z + n // 2 - step, n)
+        return lax.rem(self.z + n // 2 + step, n)
+
+    def send(self, way, step, i, fresh):
+        own = self.partial_sum(self.block_at(way, step), i)
+        if not fresh:
+            self.hop(way, step - 1, i).wait_recv()
+            own = own + self.landed[way, step - 1, i].astype(F32)
+        self.sums[way, step, i] = own.astype(BF)
+        self.hop(way, step, i).start()
+
+    def finish(self, per):
+        for j in range(self.n_z):
+            self.own_weight(j).wait()
+        self.weight_to_sibling().wait_send()
+        self.weight_from_sibling().wait_recv()
+        half = self.chunks // 2
+        for q in range(per):
+            self.gated_to_partner(q).wait_recv()
+
+        def both(step, first, fresh):
+            def body(i, carry):
+                self.send(0, step, i if first else half + i, fresh)
+                self.send(1, step, half + i if first else i, fresh)
+                return carry
+
+            lax.fori_loop(0, half, body, 0)
+
+        both(0, True, True)
+        both(1, False, True)
+        both(1, True, False)
+        steps = self.n_z // 2
+        for step in range(2, steps):
+            both(step, False, False)
+            both(step, True, False)
+
+        def home(i, carry):
+            own = self.partial_sum(self.z, i)
+            self.hop(0, steps - 1, i).wait_recv()
+            self.hop(1, steps - 1, i).wait_recv()
+            own = own + self.landed[0, steps - 1, i].astype(F32) + self.landed[1, steps - 1, i].astype(F32)
+            self.out_ref[pl.ds(pl.multiple_of(i * CHUNK, CHUNK), CHUNK), :] = own.astype(BF)
+            return carry
+
+        lax.fori_loop(0, self.chunks, home, 0)
+
+        for q in range(per):
+            self.gated_to_partner(q).wait_send()
+
+        def drain(i, carry):
+            for step in range(1, steps):
+                self.hop(0, step, i).wait_send()
+                self.hop(1, step, i).wait_send()
+            return carry
+
+        lax.fori_loop(0, self.chunks, drain, 0)
+
+        def drain_first(i, carry):
+            self.hop(0, 0, i).wait_send()
+            self.hop(1, 0, half + i).wait_send()
+            return carry
+
+        lax.fori_loop(0, half, drain_first, 0)
+
+
+def spread_scratch(n_ch, rows, depth, cols, per):
+    n_z = n_ch // 2
+    dma = pltpu.SemaphoreType.DMA
+    return [
+        pltpu.VMEM((2, n_z, depth, cols), BF),
+        pltpu.VMEM((2, rows, depth), BF),
+        pltpu.VMEM((2, n_z // 2, rows // CHUNK, CHUNK, cols), BF),
+        pltpu.VMEM((2, n_z // 2, rows // CHUNK, CHUNK, cols), BF),
+        dma((n_z,)), dma((n_z,)), dma((n_z,)), dma((2,)), dma((per,)), dma((per,)),
+        dma((2, n_z // 2, rows // CHUNK)), dma((2, n_z // 2, rows // CHUNK)),
+    ]
+
+
 def operator_kernel(
-    n_seq,
-    tok_hbm, w_hbm, taps, band, first, bias, fout, decay, outer_hbm, twist_hbm, inner_hbm, inner_back_hbm, outer_back_hbm,
-    gated_ref,
+    n_seq, n_ch,
+    tok_hbm, w_hbm, taps, band, first, bias, fout, decay, outer_hbm, twist_hbm, inner_hbm, inner_back_hbm, outer_back_hbm, wout_hbm,
+    out_ref,
     tok, w, outer, twist, inner, inner_back, outer_back,
     px, gate, halo_s, halo_r, send4, imp4, imp_recv, src_recv, conv_send, conv4,
     grid32, x_all, a_all, rows_all, imp_spec, src_spec,
-    load_sem, halo_sem, imp_ssem, imp_rsem, src_ssem, src_rsem, conv_ssem, conv_rsem, own_sem,
+    load_sem, halo_sem, imp_ssem, imp_rsem, src_ssem, src_rsem, conv_ssem, conv_rsem, *out_scratch,
 ):
     me = lax.axis_index("seq")
+    out = Spread(n_ch, wout_hbm, out_ref, *out_scratch)
     rows, width = tok_hbm.shape
     slab = w_hbm.shape[2]
     channels = slab // n_seq
@@ -111,6 +284,7 @@
     ]
     for copy in loads:
         copy.start()
+    out.load_weights()
 
     barrier = pltpu.get_barrier_semaphore()
 
@@ -119,6 +293,8 @@
         return carry
 
     lax.fori_loop(1, n_seq, greet, 0)
+    for peer in out.peers():
+        pl.semaphore_signal(barrier, inc=1, device_id=peer, device_id_type=MESH)
 
     pos = (me * rows + lax.broadcasted_iota(jnp.int32, (1, rows), 1)).astype(F32)
     scaled = pos * (1.0 / length)
@@ -144,8 +320,6 @@
     for q in range(per):
         imp4[q] = impulse[:, q * RADIX : (q + 1) * RADIX].astype(BF)
 
-    pl.semaphore_wait(barrier, n_seq - 1)
-
     def spread_copy(src, dst, ssem, rsem, peer):
         return pltpu.make_async_remote_copy(
             src_ref=src.at[:, pl.ds(pl.multiple_of(peer * channels, channels), channels), :],
@@ -176,9 +350,6 @@
 
         lax.fori_loop(1, n_seq, body, 0)
 
-    each_peer(lambda p: spread_copy(imp4, imp_recv, imp_ssem, imp_rsem, p).start())
-    own_piece(imp4, imp_recv)
-
     after = lax.rem(me + 1, n_seq)
     before = lax.rem(me + n_seq - 1, n_seq)
 
@@ -189,11 +360,10 @@
         )
 
     def project(g, part):
-        out = jnp.dot(tok[part * half : (part + 1) * half, :], w[g], preferred_element_type=F32).astype(BF)
-        px[g, 16 + part * half : 16 + (part + 1) * half, :] = out.astype(F32)
+        y = jnp.dot(tok[part * half : (part + 1) * half, :], w[g], preferred_element_type=F32).astype(BF)
+        px[g, 16 + part * half : 16 + (part + 1) * half, :] = y.astype(F32)
         if part == 1:
-            halo_s[g] = out[half - 16 :, :]
-            halo_copy(g).start()
+            halo_s[g] = y[half - 16 :, :]
 
     def take_halo(g):
         halo_copy(g).wait()
@@ -210,9 +380,19 @@
     loads[2].wait()
     project(0, 1)
     project(2, 1)
+    pl.semaphore_wait(barrier, n_seq + 2)
+    halo_copy(0).start()
+    halo_copy(2).start()
+    each_peer(lambda p: spread_copy(imp4, imp_recv, imp_ssem, imp_rsem, p).start())
+    own_piece(imp4, imp_recv)
+    out.start_weights()
     loads[3].wait()
     project(0, 0)
     project(2, 0)
+    loads[4].wait()
+    project(1, 1)
+    halo_copy(1).start()
+    project(1, 0)
     take_halo(0)
     take_halo(2)
     for q in range(per):
@@ -220,9 +400,6 @@
     each_peer(lambda p: spread_copy(send4, src_recv, src_ssem, src_rsem, p).start())
     own_piece(send4, src_recv)
 
-    loads[4].wait()
-    project(1, 1)
-    project(1, 0)
     take_halo(1)
     for q in range(per):
         gate[q * RADIX : (q + 1) * RADIX, :] = mixed(1, q)
@@ -274,17 +451,22 @@
 
     each_peer(lambda p: return_copy(p).start())
     conv4[:, pl.ds(pl.multiple_of(me * channels, channels), channels), :] = conv_send[pl.ds(me * per, per)]
+    out.pass_weights()
     each_peer(lambda p: return_arrive(p).wait_recv())
     for q in range(per):
         line = slice(q * RADIX, (q + 1) * RADIX)
-        gated_ref[line, :] = (gate[line, :] * conv4[q].astype(F32).T).astype(BF)
+        out.g2[0, line] = (gate[line, :] * conv4[q].astype(F32).T).astype(BF)
+        out.gated_to_partner(q).start()
+    out.finish(per)
 
     each_peer(lambda p: spread_copy(imp4, imp_recv, imp_ssem, imp_rsem, p).wait_send())
     each_peer(lambda p: spread_copy(send4, src_recv, src_ssem, src_rsem, p).wait_send())
     each_peer(lambda p: return_copy(p).wait_send())
 
 
-def gated_rows(n_seq, tokens, in_weight, short_taps, band_freq, filter_first, filter_bias, filter_out, decay):
+def operator_rows(
+    n_seq, n_ch, tokens, in_weight, short_taps, band_freq, filter_first, filter_bias, filter_out, decay, out_weight
+):
     rows, width = tokens.shape
     slab = in_weight.shape[2]
     channels = slab // n_seq
@@ -314,35 +496,28 @@
         pltpu.VMEM((channels * HALF, 2 * RADIX), BF),
         pltpu.VMEM((channels * HALF, 2 * RADIX), F32),
         pltpu.VMEM((channels * HALF, 2 * RADIX), F32),
-        dma((10,)), dma((2, 3)), dma((n_seq,)), dma((n_seq,)), dma((n_seq,)), dma((n_seq,)), dma((n_seq,)), dma((n_seq,)), dma,
+        dma((10,)), dma((2, 3)), dma((n_seq,)), dma((n_seq,)), dma((n_seq,)), dma((n_seq,)), dma((n_seq,)), dma((n_seq,)),
+        *spread_scratch(n_ch, rows, slab, out_weight.shape[1] // n_ch, per),
     ]
     return pl.pallas_call(
-        functools.partial(operator_kernel, n_seq),
+        functools.partial(operator_kernel, n_seq, n_ch),
         out_shape=jax.ShapeDtypeStruct((rows, slab), BF),
-        in_specs=[anyspec] * 2 + [vspec] * 6 + [anyspec] * 5,
+        in_specs=[anyspec] * 2 + [vspec] * 6 + [anyspec] * 6,
         out_specs=vspec,
         scratch_shapes=scratch,
         compiler_params=pltpu.CompilerParams(collective_id=0, has_side_effects=True, vmem_limit_bytes=56 * 2**20),
         cost_estimate=pl.CostEstimate(flops=2 * rows * width * slab * 3, bytes_accessed=12 * 2**20, transcendentals=0),
     )(
         tokens, jnp.transpose(in_weight, (1, 0, 2)), short_taps, band_freq[None, :], filter_first, filter_bias[None, :],
-        filter_out, decay[None, :], *tables,
+        filter_out, decay[None, :], *tables, out_weight,
     )
 
 
 def local(tokens, in_weight, short_taps, band_freq, filter_first, filter_bias, filter_out, decay, out_weight):
-    gated_out = gated_rows(
-        lax.axis_size("seq"), tokens, in_weight, short_taps, band_freq, filter_first, filter_bias, filter_out, decay
+    return operator_rows(
+        lax.axis_size("seq"), lax.axis_size("ch"), tokens, in_weight, short_taps, band_freq, filter_first, filter_bias,
+        filter_out, decay, out_weight,
     )
-    summed = lax.psum_scatter(
-        lax.dot_general(
-            out_weight, gated_out, (((0,), (1,)), ((), ())), preferred_element_type=jnp.float32
-        ).astype(jnp.bfloat16),
-        "ch",
-        scatter_dimension=0,
-        tiled=True,
-    ).astype(jnp.float32)
-    return summed.T.astype(jnp.bfloat16)
 
 
 def solution(mesh):

time: 146 us -> 74.4 us (0.51)
  waiting for transfers between devices: 98.3 us -> 0 us
  Pallas kernels: 28.6 us -> 72.6 us
  between operations: 13.4 us -> 0.01 us
  matrix products: 4.15 us -> 0 us
  local copies, waits for them, and re-layouts: 0.01 us -> 1.67 us
    reduce_scatter x1 -> x0, waiting for transfers between devices: 98.3 us -> none  [local(): lax.psum_scatter(lax.dot_general(out_weight, gated_out, (((0,), (1,)), ((...]
    pallas_call x1, Pallas kernels: 28.6 us -> 72.6 us  [operator_rows(): pl.pallas_call(functools.partial(operator_kernel, n_seq, n_ch), out_shape...]
    dot_general x1 -> x0, matrix products: 4.15 us -> none  [local(): lax.dot_general(out_weight, gated_out, (((0,), (1,)), ((), ())), preferre...]
    unnamed x2 -> x1, local copies, waits for them, and re-layouts: 0.01 us -> 1.67 us
  transfers between devices with their start and end apart: 1 -> 0, of which waited for: 1 -> 0; matrix products, arithmetic and copies ran while one was open for 0% -> 0% of each run, Pallas kernels for 0% -> 0%
where the time goes in v1:
time: 74.4 us; the launch traced here: 74.2 us
  Pallas kernels  72.6 us (98%)
  local copies, waits for them, and re-layouts  1.67 us (2%)
    pallas_call x1, Pallas kernels, operator_rows(): pl.pallas_call(functools.partial(operator_kernel, n_seq, n_ch), out_shape...  72.6 us
    unnamed x1, local copies, waits for them, and re-layouts  1.67 us

profile of v1, /device:TPU:1, one launch (start us, length us, event | category | flops | bytes accessed | tf_op | source)
XLA Modules:
  0.0 74.2 jit_solution(9965880737146639717)
XLA Ops:
  0.0 72.6 %shard_map.136 = bf16[512,256]{1,0:T(8,128)(2,1)} custom-call(bf16[512,4096]{1,0:T(8,128)(2,1)} %tok_hbm.1, bf16[3,4096,256]{2,1,0:T(8,128)(2,1)} %bitcast.4, f32[3,3,256]{2,1,0:T(4,128)} %taps.1, f32[1,16]{1,0:T(1,128)} %bitcast.6, f32[33,64]{1,0:T(8,128)} %first.1, f32[1,64]{1,0:T(1,128)} %bitcast.7, f32[64,256]{1,0:T(8,128)} %fout.1, f32[1,256]{1,0:T(1,128)} %bitcast.5, ...), custom_call_target="tpu_custom_call" | custom-call | flops 3221225472 | bytes 12582912 | tf_op jit(solution)/shard_map/pallas_call | solution.py:502
  72.6 1.7 %copy.16 = bf16[512,256]{1,0:T(8,128)(2,1)} copy(bf16[512,256]{1,0:T(8,128)(2,1)} %shard_map.136) | data formatting | bytes 524288

commit v2 on v1

--- a/solution.py
+++ b/solution.py
@@ -84,7 +84,7 @@
 
 
 class Spread:
-    def __init__(self, n_ch, w_hbm, out_ref, wout, g2, sums, landed, wl_sem, wx_ssem, wx_rsem, wc_sem, gx_ssem, gx_rsem, r_ssem, r_rsem):
+    def __init__(self, n_ch, w_hbm, out_ref, wout, g2, sums, landed, wl_sem, wx_ssem, wx_rsem, wc_ssem, wc_rsem, r_ssem, r_rsem):
         self.__dict__.update(locals())
         del self.__dict__["self"]
         self.n_z = n_ch // 2
@@ -93,7 +93,9 @@
         self.xl = lax.rem(self.c, 2)
         self.s = lax.axis_index("seq")
         self.core = lax.rem(self.s, 2)
-        self.partner = {"ch": self.c + 1 - 2 * self.xl}
+        self.across = self.c + 1 - 2 * self.xl
+        far = lax.rem(self.s // 2, 2)
+        self.sides = [(self.s, self.across), (self.s + 2 - 4 * far, self.across)]
         self.sibling = {"seq": self.s + 1 - 2 * self.core}
         self.up = {"ch": lax.rem(self.c + 2, n_ch)}
         self.down = {"ch": lax.rem(self.c + n_ch - 2, n_ch)}
@@ -101,9 +103,9 @@
         self.cols = w_hbm.shape[1] // n_ch
         self.rows = out_ref.shape[0]
         self.chunks = self.rows // CHUNK
-
-    def peers(self):
-        return [self.partner, self.up, self.down]
+        half = self.n_z // 2
+        shifts = [half] + [x for k in range(half - 1, 0, -1) for x in (k, self.n_z - k)] + [0]
+        self.need = [lax.rem(self.z + k, self.n_z) for k in shifts]
 
     def _columns(self, block):
         return pl.ds(pl.multiple_of(block * self.cols, self.cols), self.cols)
@@ -113,50 +115,44 @@
             self.w_hbm.at[:, self._columns(2 * j + self.xl)], self.wout.at[0, j], self.wl_sem.at[j]
         )
 
-    def weight_to_partner(self, j):
+    def weight_to_side(self, k, side):
+        j = self.need[k]
+        part = self.depth // 4
+        line = pl.ds(pl.multiple_of(self.core * 2 * part + side * part, part), part)
+        return pltpu.make_async_remote_copy(
+            src_ref=self.w_hbm.at[line, self._columns(2 * j + 1 - self.xl)],
+            dst_ref=self.wout.at[1, j, line, :],
+            send_sem=self.wx_ssem.at[side, k], recv_sem=self.wx_rsem.at[side, k],
+            device_id=self.sides[side], device_id_type=MESH,
+        )
+
+    def weight_to_sibling(self, k, core):
         half = self.depth // 2
-        part = pl.ds(pl.multiple_of(self.core * half, half), half)
-        return pltpu.make_async_remote_copy(
-            src_ref=self.w_hbm.at[part, self._columns(2 * j + 1 - self.xl)],
-            dst_ref=self.wout.at[1, j, part, :],
-            send_sem=self.wx_ssem.at[j], recv_sem=self.wx_rsem.at[j], device_id=self.partner, device_id_type=MESH,
-        )
-
-    def weight_to_sibling(self):
-        half = self.depth // 2
-        part = pl.ds(pl.multiple_of(self.core * half, half), half)
-        return pltpu.make_async_remote_copy(
-            src_ref=self.wout.at[1, :, part, :], dst_ref=self.wout.at[1, :, part, :],
-            send_sem=self.wc_sem.at[0], recv_sem=self.wc_sem.at[1], device_id=self.sibling, device_id_type=MESH,
-        )
-
-    def weight_from_sibling(self):
-        half = self.depth // 2
-        part = pl.ds(pl.multiple_of((1 - self.core) * half, half), half)
-        return pltpu.make_async_remote_copy(
-            src_ref=self.wout.at[1, :, part, :], dst_ref=self.wout.at[1, :, part, :],
-            send_sem=self.wc_sem.at[0], recv_sem=self.wc_sem.at[1], device_id=self.sibling, device_id_type=MESH,
-        )
-
-    def start_weights(self):
-        for j in range(self.n_z):
-            self.weight_to_partner(j).start()
+        piece = self.wout.at[1, self.need[k], pl.ds(pl.multiple_of(core * half, half), half), :]
+        return pltpu.make_async_remote_copy(
+            src_ref=piece, dst_ref=piece, send_sem=self.wc_ssem.at[k], recv_sem=self.wc_rsem.at[k],
+            device_id=self.sibling, device_id_type=MESH,
+        )
+
+    def start_weights(self, blocks):
+        for k in blocks:
+            for side in (0, 1):
+                self.weight_to_side(k, side).start()
 
     def load_weights(self):
         for j in range(self.n_z):
             self.own_weight(j).start()
 
-    def pass_weights(self):
-        for j in range(self.n_z):
-            self.weight_to_partner(j).wait()
-        self.weight_to_sibling().start()
-
-    def gated_to_partner(self, q):
-        line = slice(q * RADIX, (q + 1) * RADIX)
-        return pltpu.make_async_remote_copy(
-            src_ref=self.g2.at[0, line], dst_ref=self.g2.at[1, line],
-            send_sem=self.gx_ssem.at[q], recv_sem=self.gx_rsem.at[q], device_id=self.partner, device_id_type=MESH,
-        )
+    def pass_weights(self, blocks):
+        for k in blocks:
+            for side in (0, 1):
+                self.weight_to_side(k, side).wait()
+            self.weight_to_sibling(k, self.core).start()
+
+    def take_weights(self, blocks):
+        for k in blocks:
+            self.weight_to_sibling(k, self.core).wait_send()
+            self.weight_to_sibling(k, 1 - self.core).wait_recv()
 
     def hop(self, way, step, i):
         return pltpu.make_async_remote_copy(
@@ -185,14 +181,10 @@
         self.sums[way, step, i] = own.astype(BF)
         self.hop(way, step, i).start()
 
-    def finish(self, per):
+    def finish(self):
         for j in range(self.n_z):
             self.own_weight(j).wait()
-        self.weight_to_sibling().wait_send()
-        self.weight_from_sibling().wait_recv()
         half = self.chunks // 2
-        for q in range(per):
-            self.gated_to_partner(q).wait_recv()
 
         def both(step, first, fresh):
             def body(i, carry):
@@ -202,13 +194,18 @@
 
             lax.fori_loop(0, half, body, 0)
 
+        self.take_weights([0])
         both(0, True, True)
+        self.take_weights([1, 2])
         both(1, False, True)
+        self.pass_weights(range(3, self.n_z))
         both(1, True, False)
         steps = self.n_z // 2
         for step in range(2, steps):
+            self.take_weights([2 * step - 1, 2 * step])
             both(step, False, False)
             both(step, True, False)
+        self.take_weights([self.n_z - 1])
 
         def home(i, carry):
             own = self.partial_sum(self.z, i)
@@ -220,9 +217,6 @@
 
         lax.fori_loop(0, self.chunks, home, 0)
 
-        for q in range(per):
-            self.gated_to_partner(q).wait_send()
-
         def drain(i, carry):
             for step in range(1, steps):
                 self.hop(0, step, i).wait_send()
@@ -239,7 +233,7 @@
         lax.fori_loop(0, half, drain_first, 0)
 
 
-def spread_scratch(n_ch, rows, depth, cols, per):
+def spread_scratch(n_ch, rows, depth, cols):
     n_z = n_ch // 2
     dma = pltpu.SemaphoreType.DMA
     return [
@@ -247,7 +241,7 @@
         pltpu.VMEM((2, rows, depth), BF),
         pltpu.VMEM((2, n_z // 2, rows // CHUNK, CHUNK, cols), BF),
         pltpu.VMEM((2, n_z // 2, rows // CHUNK, CHUNK, cols), BF),
-        dma((n_z,)), dma((n_z,)), dma((n_z,)), dma((2,)), dma((per,)), dma((per,)),
+        dma((n_z,)), dma((2, n_z)), dma((2, n_z)), dma((n_z,)), dma((n_z,)),
         dma((2, n_z // 2, rows // CHUNK)), dma((2, n_z // 2, rows // CHUNK)),
     ]
 
@@ -257,9 +251,9 @@
     tok_hbm, w_hbm, taps, band, first, bias, fout, decay, outer_hbm, twist_hbm, inner_hbm, inner_back_hbm, outer_back_hbm, wout_hbm,
     out_ref,
     tok, w, outer, twist, inner, inner_back, outer_back,
-    px, gate, halo_s, halo_r, send4, imp4, imp_recv, src_recv, conv_send, conv4,
+    tap_cols, padded, send4, imp4, imp_recv, pro_recv, gated_send, gated,
     grid32, x_all, a_all, rows_all, imp_spec, src_spec,
-    load_sem, halo_sem, imp_ssem, imp_rsem, src_ssem, src_rsem, conv_ssem, conv_rsem, *out_scratch,
+    load_sem, imp_ssem, imp_rsem, pro_ssem, pro_rsem, gat_ssem, gat_rsem, *out_scratch,
 ):
     me = lax.axis_index("seq")
     out = Spread(n_ch, wout_hbm, out_ref, *out_scratch)
@@ -267,14 +261,15 @@
     slab = w_hbm.shape[2]
     channels = slab // n_seq
     per = rows // RADIX
+    points = per * n_seq
     half = rows // 2
     length = rows * n_seq
 
     loads = [
         pltpu.make_async_copy(w_hbm.at[0], w.at[0], load_sem.at[0]),
-        pltpu.make_async_copy(w_hbm.at[2], w.at[2], load_sem.at[1]),
+        pltpu.make_async_copy(tok_hbm.at[:half], tok.at[:half], load_sem.at[1]),
         pltpu.make_async_copy(tok_hbm.at[half:], tok.at[half:], load_sem.at[2]),
-        pltpu.make_async_copy(tok_hbm.at[:half], tok.at[:half], load_sem.at[3]),
+        pltpu.make_async_copy(w_hbm.at[2], w.at[2], load_sem.at[3]),
         pltpu.make_async_copy(w_hbm.at[1], w.at[1], load_sem.at[4]),
         pltpu.make_async_copy(outer_hbm, outer, load_sem.at[5]),
         pltpu.make_async_copy(twist_hbm, twist, load_sem.at[6]),
@@ -293,7 +288,13 @@
         return carry
 
     lax.fori_loop(1, n_seq, greet, 0)
-    for peer in out.peers():
+
+    def greet_across(p, carry):
+        pl.semaphore_signal(barrier, inc=1, device_id=(p, out.across), device_id_type=MESH)
+        return carry
+
+    lax.fori_loop(0, n_seq, greet_across, 0)
+    for peer in (out.up, out.down):
         pl.semaphore_signal(barrier, inc=1, device_id=peer, device_id_type=MESH)
 
     pos = (me * rows + lax.broadcasted_iota(jnp.int32, (1, rows), 1)).astype(F32)
@@ -320,6 +321,13 @@
     for q in range(per):
         imp4[q] = impulse[:, q * RADIX : (q + 1) * RADIX].astype(BF)
 
+    for g in range(3):
+        for i in range(3):
+            tap_cols[g, i] = jnp.broadcast_to(taps[i, g : g + 1, :], (RADIX, slab)).T
+        padded[g, 0:channels, :] = jnp.zeros((channels, RADIX), F32)
+
+    mine = pl.ds(pl.multiple_of(me * channels, channels), channels)
+
     def spread_copy(src, dst, ssem, rsem, peer):
         return pltpu.make_async_remote_copy(
             src_ref=src.at[:, pl.ds(pl.multiple_of(peer * channels, channels), channels), :],
@@ -331,17 +339,14 @@
         )
 
     def arrive(dst, ssem, rsem, peer):
-        return pltpu.make_async_remote_copy(
-            src_ref=dst.at[pl.ds(peer * per, per)],
-            dst_ref=dst.at[pl.ds(peer * per, per)],
-            send_sem=ssem.at[peer],
-            recv_sem=rsem.at[peer],
-            device_id={"seq": peer},
-            device_id_type=MESH,
+        piece = dst.at[pl.ds(peer * per, per)]
+        return pltpu.make_async_remote_copy(
+            src_ref=piece, dst_ref=piece, send_sem=ssem.at[peer], recv_sem=rsem.at[peer],
+            device_id={"seq": peer}, device_id_type=MESH,
         )
 
     def own_piece(src, dst):
-        dst[pl.ds(me * per, per)] = src[:, pl.ds(pl.multiple_of(me * channels, channels), channels), :]
+        dst[pl.ds(me * per, per)] = src[:, mine, :]
 
     def each_peer(step):
         def body(d, carry):
@@ -350,69 +355,70 @@
 
         lax.fori_loop(1, n_seq, body, 0)
 
-    after = lax.rem(me + 1, n_seq)
-    before = lax.rem(me + n_seq - 1, n_seq)
-
-    def halo_copy(g):
-        return pltpu.make_async_remote_copy(
-            src_ref=halo_s.at[g], dst_ref=halo_r.at[g], send_sem=halo_sem.at[0, g], recv_sem=halo_sem.at[1, g],
-            device_id={"seq": after}, device_id_type=MESH,
-        )
-
-    def project(g, part):
-        y = jnp.dot(tok[part * half : (part + 1) * half, :], w[g], preferred_element_type=F32).astype(BF)
-        px[g, 16 + part * half : 16 + (part + 1) * half, :] = y.astype(F32)
-        if part == 1:
-            halo_s[g] = y[half - 16 :, :]
-
-    def take_halo(g):
-        halo_copy(g).wait()
-        px[g, 0:16, :] = jnp.where(me > 0, halo_r[g].astype(F32), 0.0)
-
-    def mixed(g, q):
-        total = taps[0, g : g + 1, :] * px[g, 16 + q * RADIX : 16 + (q + 1) * RADIX, :]
-        for i in (1, 2):
-            total = total + taps[i, g : g + 1, :] * px[g, 16 - i + q * RADIX : 16 - i + (q + 1) * RADIX, :]
-        return total
+    def project(g):
+        for part in (0, 1):
+            if g == 0:
+                loads[1 + part].wait()
+            y = jnp.dot(tok[part * half : (part + 1) * half, :], w[g], preferred_element_type=F32)
+            for q in range(per // 2):
+                send4[g, part * (per // 2) + q] = y[q * RADIX : (q + 1) * RADIX, :].T.astype(BF)
+
+    def project_copy(g, p):
+        return spread_copy(send4.at[g], pro_recv.at[g], pro_ssem.at[g], pro_rsem.at[g], p)
+
+    def mixed(g, row, count):
+        lane = lax.broadcasted_iota(jnp.int32, (count, RADIX), 1)
+        now = padded[g, pl.ds(channels + row, count), :]
+        before = padded[g, pl.ds(row, count), :]
+        total = jnp.zeros((count // channels, channels, RADIX), F32)
+        for i in range(3):
+            moved = now if i == 0 else pltpu.roll(jnp.where(lane >= RADIX - i, before, now), i, 1)
+            total = total + tap_cols[g, i, mine, :][None] * moved.reshape(count // channels, channels, RADIX)
+        return total.reshape(count, RADIX)
+
+    def take_projected(g):
+        each_peer(lambda p: arrive(pro_recv.at[g], pro_ssem.at[g], pro_rsem.at[g], p).wait_recv())
+        padded[g, channels:, :] = pro_recv[g].astype(F32).reshape(points * channels, RADIX)
+
+    block = 8 * channels
+
+    def each_block(step):
+        def body(i, carry):
+            step(pl.multiple_of(i * block, block))
+            return carry
+
+        lax.fori_loop(0, points * channels // block, body, 0)
 
     loads[0].wait()
-    loads[1].wait()
-    loads[2].wait()
-    project(0, 1)
-    project(2, 1)
-    pl.semaphore_wait(barrier, n_seq + 2)
-    halo_copy(0).start()
-    halo_copy(2).start()
+    project(0)
+    pl.semaphore_wait(barrier, 2 * n_seq + 1)
+    each_peer(lambda p: project_copy(0, p).start())
+    loads[3].wait()
+    project(2)
+    each_peer(lambda p: project_copy(2, p).start())
     each_peer(lambda p: spread_copy(imp4, imp_recv, imp_ssem, imp_rsem, p).start())
+    out.start_weights(range(3))
+    loads[4].wait()
+    project(1)
+    each_peer(lambda p: project_copy(1, p).start())
+    out.start_weights(range(3, out.n_z))
     own_piece(imp4, imp_recv)
-    out.start_weights()
-    loads[3].wait()
-    project(0, 0)
-    project(2, 0)
-    loads[4].wait()
-    project(1, 1)
-    halo_copy(1).start()
-    project(1, 0)
-    take_halo(0)
-    take_halo(2)
-    for q in range(per):
-        send4[q] = (mixed(0, q) * mixed(2, q)).T.astype(BF)
-    each_peer(lambda p: spread_copy(send4, src_recv, src_ssem, src_rsem, p).start())
-    own_piece(send4, src_recv)
-
-    take_halo(1)
-    for q in range(per):
-        gate[q * RADIX : (q + 1) * RADIX, :] = mixed(1, q)
-
+    for g in range(3):
+        own_piece(send4.at[g], pro_recv.at[g])
     for copy in loads[5:]:
         copy.wait()
+
     each_peer(lambda p: arrive(imp_recv, imp_ssem, imp_rsem, p).wait_recv())
-    points = per * n_seq
     grid32[...] = imp_recv[...].astype(F32).reshape(points * channels, RADIX)
     forward(grid32, x_all, a_all, rows_all, outer, twist, inner, imp_spec, channels)
 
-    each_peer(lambda p: arrive(src_recv, src_ssem, src_rsem, p).wait_recv())
-    grid32[...] = src_recv[...].astype(F32).reshape(points * channels, RADIX)
+    take_projected(0)
+    take_projected(2)
+
+    def source_block(row):
+        grid32[pl.ds(row, block), :] = mixed(0, row, block) * mixed(2, row, block)
+
+    each_block(source_block)
     forward(grid32, x_all, a_all, rows_all, outer, twist, inner, src_spec, channels)
 
     for c in range(channels):
@@ -430,38 +436,53 @@
         back = jnp.concatenate([re * co - im * si, im * co + re * si], 0).astype(BF)
         y = jnp.dot(outer_back[...], back, preferred_element_type=F32)
         grid32[pl.ds(c, points, stride=channels), :] = y
-    conv_send[...] = grid32[...].astype(BF).reshape(points, channels, RADIX)
-
-    def return_copy(peer):
-        return pltpu.make_async_remote_copy(
-            src_ref=conv_send.at[pl.ds(peer * per, per)],
-            dst_ref=conv4.at[:, pl.ds(pl.multiple_of(me * channels, channels), channels), :],
-            send_sem=conv_ssem.at[peer],
-            recv_sem=conv_rsem.at[me],
-            device_id={"seq": peer},
+    take_projected(1)
+
+    def gate_block(row):
+        value = grid32[pl.ds(row, block), :] * mixed(1, row, block)
+        gated_send[pl.ds(row // channels, 8)] = value.astype(BF).reshape(8, channels, RADIX)
+
+    each_block(gate_block)
+
+    def gated_copy(side, peer):
+        return pltpu.make_async_remote_copy(
+            src_ref=gated_send.at[pl.ds(peer * per, per)],
+            dst_ref=gated.at[side, :, mine, :],
+            send_sem=gat_ssem.at[side, peer],
+            recv_sem=gat_rsem.at[side, me],
+            device_id=(peer, out.across if side else out.c),
             device_id_type=MESH,
         )
 
-    def return_arrive(peer):
-        piece = conv4.at[:, pl.ds(pl.multiple_of(peer * channels, channels), channels), :]
-        return pltpu.make_async_remote_copy(
-            src_ref=piece, dst_ref=piece, send_sem=conv_ssem.at[peer], recv_sem=conv_rsem.at[peer],
-            device_id={"seq": peer}, device_id_type=MESH,
-        )
-
-    each_peer(lambda p: return_copy(p).start())
-    conv4[:, pl.ds(pl.multiple_of(me * channels, channels), channels), :] = conv_send[pl.ds(me * per, per)]
-    out.pass_weights()
-    each_peer(lambda p: return_arrive(p).wait_recv())
-    for q in range(per):
-        line = slice(q * RADIX, (q + 1) * RADIX)
-        out.g2[0, line] = (gate[line, :] * conv4[q].astype(F32).T).astype(BF)
-        out.gated_to_partner(q).start()
-    out.finish(per)
+    def gated_arrive(side, peer):
+        piece = gated.at[side, :, pl.ds(pl.multiple_of(peer * channels, channels), channels), :]
+        return pltpu.make_async_remote_copy(
+            src_ref=piece, dst_ref=piece, send_sem=gat_ssem.at[side, peer], recv_sem=gat_rsem.at[side, peer],
+            device_id=(peer, out.across if side else out.c), device_id_type=MESH,
+        )
+
+    def both_sides(p):
+        gated_copy(0, p).start()
+        gated_copy(1, p).start()
+
+    each_peer(both_sides)
+    gated_copy(1, me).start()
+    gated[0, :, mine, :] = gated_send[pl.ds(me * per, per)]
+    out.pass_weights(range(3))
+    for side in (0, 1):
+        each_peer(lambda p: gated_arrive(side, p).wait_recv())
+        if side:
+            gated_arrive(1, me).wait_recv()
+        for q in range(per):
+            out.g2[side, q * RADIX : (q + 1) * RADIX, :] = gated[side, q].astype(F32).T.astype(BF)
+    out.finish()
 
     each_peer(lambda p: spread_copy(imp4, imp_recv, imp_ssem, imp_rsem, p).wait_send())
-    each_peer(lambda p: spread_copy(send4, src_recv, src_ssem, src_rsem, p).wait_send())
-    each_peer(lambda p: return_copy(p).wait_send())
+    for g in range(3):
+        each_peer(lambda p: project_copy(g, p).wait_send())
+    for side in (0, 1):
+        each_peer(lambda p: gated_copy(side, p).wait_send())
+    gated_copy(1, me).wait_send()
 
 
 def operator_rows(
@@ -480,24 +501,22 @@
         pltpu.VMEM((rows, width), BF),
         pltpu.VMEM((3, width, slab), BF),
         *[pltpu.VMEM(t.shape, t.dtype) for t in tables],
-        pltpu.VMEM((3, rows + 16, slab), F32),
-        pltpu.VMEM((rows, slab), F32),
-        pltpu.VMEM((3, 16, slab), BF),
-        pltpu.VMEM((3, 16, slab), BF),
-        pltpu.VMEM((per, slab, RADIX), BF),
+        pltpu.VMEM((3, 3, slab, RADIX), F32),
+        pltpu.VMEM((3, (points + 1) * channels, RADIX), F32),
+        pltpu.VMEM((3, per, slab, RADIX), BF),
         pltpu.VMEM((per, slab, RADIX), BF),
         pltpu.VMEM((points, channels, RADIX), BF),
+        pltpu.VMEM((3, points, channels, RADIX), BF),
         pltpu.VMEM((points, channels, RADIX), BF),
-        pltpu.VMEM((points, channels, RADIX), BF),
-        pltpu.VMEM((per, slab, RADIX), BF),
+        pltpu.VMEM((2, per, slab, RADIX), BF),
         pltpu.VMEM((points * channels, RADIX), F32),
         pltpu.VMEM((points, channels * RADIX), BF),
         pltpu.VMEM((2 * HALF, channels * RADIX), F32),
         pltpu.VMEM((channels * HALF, 2 * RADIX), BF),
         pltpu.VMEM((channels * HALF, 2 * RADIX), F32),
         pltpu.VMEM((channels * HALF, 2 * RADIX), F32),
-        dma((10,)), dma((2, 3)), dma((n_seq,)), dma((n_seq,)), dma((n_seq,)), dma((n_seq,)), dma((n_seq,)), dma((n_seq,)),
-        *spread_scratch(n_ch, rows, slab, out_weight.shape[1] // n_ch, per),
+        dma((10,)), dma((n_seq,)), dma((n_seq,)), dma((3, n_seq)), dma((3, n_seq)), dma((2, n_seq)), dma((2, n_seq)),
+        *spread_scratch(n_ch, rows, slab, out_weight.shape[1] // n_ch),
     ]
     return pl.pallas_call(
         functools.partial(operator_kernel, n_seq, n_ch),

time: 74.4 us -> 69.9 us (0.940)
  Pallas kernels: 72.6 us -> 68 us
    pallas_call x1, Pallas kernels: 72.6 us -> 68 us  [operator_rows(): pl.pallas_call(functools.partial(operator_kernel, n_seq, n_ch), out_shape...]
where the time goes in v2:
time: 69.9 us; the launch traced here: 69.7 us
  Pallas kernels  68 us (97%)
  local copies, waits for them, and re-layouts  1.67 us (2%)
    pallas_call x1, Pallas kernels, operator_rows(): pl.pallas_call(functools.partial(operator_kernel, n_seq, n_ch), out_shape...  68 us
    unnamed x1, local copies, waits for them, and re-layouts  1.67 us

profile of v2, /device:TPU:1, one launch (start us, length us, event | category | flops | bytes accessed | tf_op | source)
XLA Modules:
  0.0 69.7 jit_solution(11582926850677888419)
XLA Ops:
  0.0 68.0 %shard_map.136 = bf16[512,256]{1,0:T(8,128)(2,1)} custom-call(bf16[512,4096]{1,0:T(8,128)(2,1)} %tok_hbm.1, bf16[3,4096,256]{2,1,0:T(8,128)(2,1)} %bitcast.4, f32[3,3,256]{2,1,0:T(4,128)} %taps.1, f32[1,16]{1,0:T(1,128)} %bitcast.6, f32[33,64]{1,0:T(8,128)} %first.1, f32[1,64]{1,0:T(1,128)} %bitcast.7, f32[64,256]{1,0:T(8,128)} %fout.1, f32[1,256]{1,0:T(1,128)} %bitcast.5, ...), custom_call_target="tpu_custom_call" | custom-call | flops 3221225472 | bytes 12582912 | tf_op jit(solution)/shard_map/pallas_call | solution.py:521
  68.0 1.7 %copy.16 = bf16[512,256]{1,0:T(8,128)(2,1)} copy(bf16[512,256]{1,0:T(8,128)(2,1)} %shard_map.136) | data formatting | bytes 524288

commit v3 on v2

--- a/solution.py
+++ b/solution.py
@@ -181,30 +181,31 @@
         self.sums[way, step, i] = own.astype(BF)
         self.hop(way, step, i).start()
 
-    def finish(self):
+    def finish(self, take_gated):
         for j in range(self.n_z):
             self.own_weight(j).wait()
         half = self.chunks // 2
 
-        def both(step, first, fresh):
+        def both(steps, firsts, fresh):
             def body(i, carry):
-                self.send(0, step, i if first else half + i, fresh)
-                self.send(1, step, half + i if first else i, fresh)
+                for way in (0, 1):
+                    self.send(way, steps[way], i if firsts[way] else half + i, fresh)
                 return carry
 
             lax.fori_loop(0, half, body, 0)
 
-        self.take_weights([0])
-        both(0, True, True)
-        self.take_weights([1, 2])
-        both(1, False, True)
+        self.take_weights([0, 1, 2])
+        take_gated(0)
+        both((0, 1), (True, True), True)
+        take_gated(1)
+        both((1, 0), (False, False), True)
         self.pass_weights(range(3, self.n_z))
-        both(1, True, False)
+        both((1, 1), (True, False), False)
         steps = self.n_z // 2
         for step in range(2, steps):
             self.take_weights([2 * step - 1, 2 * step])
-            both(step, False, False)
-            both(step, True, False)
+            both((step, step), (False, True), False)
+            both((step, step), (True, False), False)
         self.take_weights([self.n_z - 1])
 
         def home(i, carry):
@@ -251,9 +252,9 @@
     tok_hbm, w_hbm, taps, band, first, bias, fout, decay, outer_hbm, twist_hbm, inner_hbm, inner_back_hbm, outer_back_hbm, wout_hbm,
     out_ref,
     tok, w, outer, twist, inner, inner_back, outer_back,
-    tap_cols, padded, send4, imp4, imp_recv, pro_recv, gated_send, gated,
+    tap_cols, fout_rows, decay_cols, padded, send4, pro_recv, gated_send, gated,
     grid32, x_all, a_all, rows_all, imp_spec, src_spec,
-    load_sem, imp_ssem, imp_rsem, pro_ssem, pro_rsem, gat_ssem, gat_rsem, *out_scratch,
+    load_sem, pro_ssem, pro_rsem, gat_ssem, gat_rsem, *out_scratch,
 ):
     me = lax.axis_index("seq")
     out = Spread(n_ch, wout_hbm, out_ref, *out_scratch)
@@ -279,7 +280,6 @@
     ]
     for copy in loads:
         copy.start()
-    out.load_weights()
 
     barrier = pltpu.get_barrier_semaphore()
 
@@ -296,35 +296,13 @@
     lax.fori_loop(0, n_seq, greet_across, 0)
     for peer in (out.up, out.down):
         pl.semaphore_signal(barrier, inc=1, device_id=peer, device_id_type=MESH)
-
-    pos = (me * rows + lax.broadcasted_iota(jnp.int32, (1, rows), 1)).astype(F32)
-    scaled = pos * (1.0 / length)
-    turns = outer_product(band[...], scaled)
-    turns = turns - jnp.round(turns)
-    n_band = band.shape[1]
-    head = lax.broadcasted_iota(jnp.int32, (8, rows), 0)
-    features = jnp.concatenate(
-        [sin_turns(turns + 0.25), sin_turns(turns), jnp.where(head == 0, scaled, jnp.where(head == 1, 1.0, 0.0))], 0
-    )
-    head = lax.broadcasted_iota(jnp.int32, (8, first.shape[1]), 0)
-    layer = jnp.concatenate(
-        [
-            first[1 : 1 + n_band, :],
-            first[1 + n_band :, :],
-            jnp.where(head == 0, first[0:1, :], jnp.where(head == 1, bias[...], 0.0)),
-        ],
-        0,
-    )
-    pre = contract_rows(layer, features)
-    hidden = sin_turns(pre * (1.0 / (2.0 * math.pi)))
-    impulse = contract_rows(fout[...], hidden) * jnp.exp(-outer_product(decay[...], pos))
-    for q in range(per):
-        imp4[q] = impulse[:, q * RADIX : (q + 1) * RADIX].astype(BF)
 
     for g in range(3):
         for i in range(3):
             tap_cols[g, i] = jnp.broadcast_to(taps[i, g : g + 1, :], (RADIX, slab)).T
         padded[g, 0:channels, :] = jnp.zeros((channels, RADIX), F32)
+    fout_rows[...] = fout[...].T
+    decay_cols[...] = jnp.broadcast_to(decay[...], (RADIX, slab)).T
 
     mine = pl.ds(pl.multiple_of(me * channels, channels), channels)
 
@@ -389,6 +367,36 @@
 
         lax.fori_loop(0, points * channels // block, body, 0)
 
+    n_band = band.shape[1]
+    stretch = 2 * rows
+
+    def filter_block(step, carry):
+        pos = (step * stretch + lax.broadcasted_iota(jnp.int32, (1, stretch), 1)).astype(F32)
+        scaled = pos * (1.0 / length)
+        turns = outer_product(band[...], scaled)
+        turns = turns - jnp.round(turns)
+        head = lax.broadcasted_iota(jnp.int32, (8, stretch), 0)
+        features = jnp.concatenate(
+            [sin_turns(turns + 0.25), sin_turns(turns), jnp.where(head == 0, scaled, jnp.where(head == 1, 1.0, 0.0))], 0
+        )
+        head = lax.broadcasted_iota(jnp.int32, (8, first.shape[1]), 0)
+        layer = jnp.concatenate(
+            [
+                first[1 : 1 + n_band, :],
+                first[1 + n_band :, :],
+                jnp.where(head == 0, first[0:1, :], jnp.where(head == 1, bias[...], 0.0)),
+            ],
+            0,
+        )
+        hidden = sin_turns(contract_rows(layer, features) * (1.0 / (2.0 * math.pi)))
+        shaped = jnp.dot(fout_rows[mine, :], hidden, precision=HIGH, preferred_element_type=F32)
+        fall = -decay_cols[mine, :]
+        for q in range(stretch // RADIX):
+            lanes = slice(q * RADIX, (q + 1) * RADIX)
+            row = pl.multiple_of((step * (stretch // RADIX) + q) * channels, channels)
+            grid32[pl.ds(row, channels), :] = shaped[:, lanes] * jnp.exp(fall * pos[:, lanes])
+        return carry
+
     loads[0].wait()
     project(0)
     pl.semaphore_wait(barrier, 2 * n_seq + 1)
@@ -396,20 +404,18 @@
     loads[3].wait()
     project(2)
     each_peer(lambda p: project_copy(2, p).start())
-    each_peer(lambda p: spread_copy(imp4, imp_recv, imp_ssem, imp_rsem, p).start())
     out.start_weights(range(3))
     loads[4].wait()
     project(1)
     each_peer(lambda p: project_copy(1, p).start())
     out.start_weights(range(3, out.n_z))
-    own_piece(imp4, imp_recv)
+    out.load_weights()
     for g in range(3):
         own_piece(send4.at[g], pro_recv.at[g])
     for copy in loads[5:]:
         copy.wait()
 
-    each_peer(lambda p: arrive(imp_recv, imp_ssem, imp_rsem, p).wait_recv())
-    grid32[...] = imp_recv[...].astype(F32).reshape(points * channels, RADIX)
+    lax.fori_loop(0, length // stretch, filter_block, 0)
     forward(grid32, x_all, a_all, rows_all, outer, twist, inner, imp_spec, channels)
 
     take_projected(0)
@@ -444,45 +450,54 @@
 
     each_block(gate_block)
 
-    def gated_copy(side, peer):
-        return pltpu.make_async_remote_copy(
-            src_ref=gated_send.at[pl.ds(peer * per, per)],
-            dst_ref=gated.at[side, :, mine, :],
-            send_sem=gat_ssem.at[side, peer],
-            recv_sem=gat_rsem.at[side, me],
+    few = per // 2
+
+    def gated_copy(side, part, peer):
+        return pltpu.make_async_remote_copy(
+            src_ref=gated_send.at[pl.ds(peer * per + part * few, few)],
+            dst_ref=gated.at[side, part * few : (part + 1) * few, mine, :],
+            send_sem=gat_ssem.at[side, part, peer],
+            recv_sem=gat_rsem.at[side, part, me],
             device_id=(peer, out.across if side else out.c),
             device_id_type=MESH,
         )
 
-    def gated_arrive(side, peer):
-        piece = gated.at[side, :, pl.ds(pl.multiple_of(peer * channels, channels), channels), :]
-        return pltpu.make_async_remote_copy(
-            src_ref=piece, dst_ref=piece, send_sem=gat_ssem.at[side, peer], recv_sem=gat_rsem.at[side, peer],
+    def gated_arrive(side, part, peer):
+        piece = gated.at[
+            side, part * few : (part + 1) * few, pl.ds(pl.multiple_of(peer * channels, channels), channels), :
+        ]
+        return pltpu.make_async_remote_copy(
+            src_ref=piece, dst_ref=piece, send_sem=gat_ssem.at[side, part, peer], recv_sem=gat_rsem.at[side, part, peer],
             device_id=(peer, out.across if side else out.c), device_id_type=MESH,
         )
 
-    def both_sides(p):
-        gated_copy(0, p).start()
-        gated_copy(1, p).start()
-
-    each_peer(both_sides)
-    gated_copy(1, me).start()
+    for part in (0, 1):
+
+        def both_sides(p):
+            gated_copy(0, part, p).start()
+            gated_copy(1, part, p).start()
+
+        each_peer(both_sides)
+        gated_copy(1, part, me).start()
     gated[0, :, mine, :] = gated_send[pl.ds(me * per, per)]
     out.pass_weights(range(3))
-    for side in (0, 1):
-        each_peer(lambda p: gated_arrive(side, p).wait_recv())
-        if side:
-            gated_arrive(1, me).wait_recv()
-        for q in range(per):
-            out.g2[side, q * RADIX : (q + 1) * RADIX, :] = gated[side, q].astype(F32).T.astype(BF)
-    out.finish()
-
-    each_peer(lambda p: spread_copy(imp4, imp_recv, imp_ssem, imp_rsem, p).wait_send())
+
+    def take_gated(part):
+        for side in (0, 1):
+            each_peer(lambda p: gated_arrive(side, part, p).wait_recv())
+            if side:
+                gated_arrive(1, part, me).wait_recv()
+            for q in range(part * few, (part + 1) * few):
+                out.g2[side, q * RADIX : (q + 1) * RADIX, :] = gated[side, q].astype(F32).T.astype(BF)
+
+    out.finish(take_gated)
+
     for g in range(3):
         each_peer(lambda p: project_copy(g, p).wait_send())
-    for side in (0, 1):
-        each_peer(lambda p: gated_copy(side, p).wait_send())
-    gated_copy(1, me).wait_send()
+    for part in (0, 1):
+        for side in (0, 1):
+            each_peer(lambda p: gated_copy(side, part, p).wait_send())
+        gated_copy(1, part, me).wait_send()
 
 
 def operator_rows(
@@ -502,10 +517,10 @@
         pltpu.VMEM((3, width, slab), BF),
         *[pltpu.VMEM(t.shape, t.dtype) for t in tables],
         pltpu.VMEM((3, 3, slab, RADIX), F32),
+        pltpu.VMEM((slab, filter_out.shape[0]), F32),
+        pltpu.VMEM((slab, RADIX), F32),
         pltpu.VMEM((3, (points + 1) * channels, RADIX), F32),
         pltpu.VMEM((3, per, slab, RADIX), BF),
-        pltpu.VMEM((per, slab, RADIX), BF),
-        pltpu.VMEM((points, channels, RADIX), BF),
         pltpu.VMEM((3, points, channels, RADIX), BF),
         pltpu.VMEM((points, channels, RADIX), BF),
         pltpu.VMEM((2, per, slab, RADIX), BF),
@@ -515,7 +530,7 @@
         pltpu.VMEM((channels * HALF, 2 * RADIX), BF),
         pltpu.VMEM((channels * HALF, 2 * RADIX), F32),
         pltpu.VMEM((channels * HALF, 2 * RADIX), F32),
-        dma((10,)), dma((n_seq,)), dma((n_seq,)), dma((3, n_seq)), dma((3, n_seq)), dma((2, n_seq)), dma((2, n_seq)),
+        dma((10,)), dma((3, n_seq)), dma((3, n_seq)), dma((2, 2, n_seq)), dma((2, 2, n_seq)),
         *spread_scratch(n_ch, rows, slab, out_weight.shape[1] // n_ch),
     ]
     return pl.pallas_call(

time: 69.9 us -> 66 us (0.944)
  Pallas kernels: 68 us -> 64.2 us
    pallas_call x1, Pallas kernels: 68 us -> 64.2 us  [operator_rows(): pl.pallas_call(functools.partial(operator_kernel, n_seq, n_ch), out_shape...]
where the time goes in v3:
time: 66 us; the launch traced here: 65.8 us
  Pallas kernels  64.2 us (97%)
  local copies, waits for them, and re-layouts  1.67 us (3%)
    pallas_call x1, Pallas kernels, operator_rows(): pl.pallas_call(functools.partial(operator_kernel, n_seq, n_ch), out_shape...  64.2 us
    unnamed x1, local copies, waits for them, and re-layouts  1.67 us

profile of v3, /device:TPU:1, one launch (start us, length us, event | category | flops | bytes accessed | tf_op | source)
XLA Modules:
  0.0 65.8 jit_solution(10540566515117473541)
XLA Ops:
  0.0 64.2 %shard_map.136 = bf16[512,256]{1,0:T(8,128)(2,1)} custom-call(bf16[512,4096]{1,0:T(8,128)(2,1)} %tok_hbm.1, bf16[3,4096,256]{2,1,0:T(8,128)(2,1)} %bitcast.4, f32[3,3,256]{2,1,0:T(4,128)} %taps.1, f32[1,16]{1,0:T(1,128)} %bitcast.6, f32[33,64]{1,0:T(8,128)} %first.1, f32[1,64]{1,0:T(1,128)} %bitcast.7, f32[64,256]{1,0:T(8,128)} %fout.1, f32[1,256]{1,0:T(1,128)} %bitcast.5, ...), custom_call_target="tpu_custom_call" | custom-call | flops 3221225472 | bytes 12582912 | tf_op jit(solution)/shard_map/pallas_call | solution.py:536
  64.2 1.7 %copy.16 = bf16[512,256]{1,0:T(8,128)(2,1)} copy(bf16[512,256]{1,0:T(8,128)(2,1)} %shard_map.136) | data formatting | bytes 524288

commit v4 on v3

--- a/solution.py
+++ b/solution.py
@@ -80,7 +80,7 @@
     spec_ref[...] = jnp.dot(rows_all[...], inner[...], preferred_element_type=F32)
 
 
-CHUNK = 64
+CHUNK = 256
 
 
 class Spread:
@@ -308,7 +308,7 @@
 
     def spread_copy(src, dst, ssem, rsem, peer):
         return pltpu.make_async_remote_copy(
-            src_ref=src.at[:, pl.ds(pl.multiple_of(peer * channels, channels), channels), :],
+            src_ref=src.at[peer],
             dst_ref=dst.at[pl.ds(me * per, per)],
             send_sem=ssem.at[peer],
             recv_sem=rsem.at[me],
@@ -324,7 +324,7 @@
         )
 
     def own_piece(src, dst):
-        dst[pl.ds(me * per, per)] = src[:, mine, :]
+        dst[pl.ds(me * per, per)] = src[me]
 
     def each_peer(step):
         def body(d, carry):
@@ -339,7 +339,8 @@
                 loads[1 + part].wait()
             y = jnp.dot(tok[part * half : (part + 1) * half, :], w[g], preferred_element_type=F32)
             for q in range(per // 2):
-                send4[g, part * (per // 2) + q] = y[q * RADIX : (q + 1) * RADIX, :].T.astype(BF)
+                piece = y[q * RADIX : (q + 1) * RADIX, :].T.astype(BF)
+                send4[g, :, part * (per // 2) + q] = piece.reshape(n_seq, channels, RADIX)
 
     def project_copy(g, p):
         return spread_copy(send4.at[g], pro_recv.at[g], pro_ssem.at[g], pro_rsem.at[g], p)
@@ -455,7 +456,7 @@
     def gated_copy(side, part, peer):
         return pltpu.make_async_remote_copy(
             src_ref=gated_send.at[pl.ds(peer * per + part * few, few)],
-            dst_ref=gated.at[side, part * few : (part + 1) * few, mine, :],
+            dst_ref=gated.at[side, me, part * few : (part + 1) * few],
             send_sem=gat_ssem.at[side, part, peer],
             recv_sem=gat_rsem.at[side, part, me],
             device_id=(peer, out.across if side else out.c),
@@ -463,9 +464,7 @@
         )
 
     def gated_arrive(side, part, peer):
-        piece = gated.at[
-            side, part * few : (part + 1) * few, pl.ds(pl.multiple_of(peer * channels, channels), channels), :
-        ]
+        piece = gated.at[side, peer, part * few : (part + 1) * few]
         return pltpu.make_async_remote_copy(
             src_ref=piece, dst_ref=piece, send_sem=gat_ssem.at[side, part, peer], recv_sem=gat_rsem.at[side, part, peer],
             device_id=(peer, out.across if side else out.c), device_id_type=MESH,
@@ -479,7 +478,7 @@
 
         each_peer(both_sides)
         gated_copy(1, part, me).start()
-    gated[0, :, mine, :] = gated_send[pl.ds(me * per, per)]
+    gated[0, me] = gated_send[pl.ds(me * per, per)]
     out.pass_weights(range(3))
 
     def take_gated(part):
@@ -488,7 +487,8 @@
             if side:
                 gated_arrive(1, part, me).wait_recv()
             for q in range(part * few, (part + 1) * few):
-                out.g2[side, q * RADIX : (q + 1) * RADIX, :] = gated[side, q].astype(F32).T.astype(BF)
+                rows_first = gated[side, :, q].reshape(slab, RADIX).astype(F32)
+                out.g2[side, q * RADIX : (q + 1) * RADIX, :] = rows_first.T.astype(BF)
 
     out.finish(take_gated)
 
@@ -520,10 +520,10 @@
         pltpu.VMEM((slab, filter_out.shape[0]), F32),
         pltpu.VMEM((slab, RADIX), F32),
         pltpu.VMEM((3, (points + 1) * channels, RADIX), F32),
-        pltpu.VMEM((3, per, slab, RADIX), BF),
+        pltpu.VMEM((3, n_seq, per, channels, RADIX), BF),
         pltpu.VMEM((3, points, channels, RADIX), BF),
         pltpu.VMEM((points, channels, RADIX), BF),
-        pltpu.VMEM((2, per, slab, RADIX), BF),
+        pltpu.VMEM((2, n_seq, per, channels, RADIX), BF),
         pltpu.VMEM((points * channels, RADIX), F32),
         pltpu.VMEM((points, channels * RADIX), BF),
         pltpu.VMEM((2 * HALF, channels * RADIX), F32),

time: 66 us -> 64.2 us (0.973)
  Pallas kernels: 64.2 us -> 62.3 us
    pallas_call x1, Pallas kernels: 64.2 us -> 62.3 us  [operator_rows(): pl.pallas_call(functools.partial(operator_kernel, n_seq, n_ch), out_shape...]
where the time goes in v4:
time: 64.2 us; the launch traced here: 64 us
  Pallas kernels  62.3 us (97%)
  local copies, waits for them, and re-layouts  1.67 us (3%)
    pallas_call x1, Pallas kernels, operator_rows(): pl.pallas_call(functools.partial(operator_kernel, n_seq, n_ch), out_shape...  62.3 us
    unnamed x1, local copies, waits for them, and re-layouts  1.67 us

profile of v4, /device:TPU:1, one launch (start us, length us, event | category | flops | bytes accessed | tf_op | source)
XLA Modules:
  0.0 64.0 jit_solution(12593899840940830322)
XLA Ops:
  0.0 62.3 %shard_map.136 = bf16[512,256]{1,0:T(8,128)(2,1)} custom-call(bf16[512,4096]{1,0:T(8,128)(2,1)} %tok_hbm.1, bf16[3,4096,256]{2,1,0:T(8,128)(2,1)} %bitcast.4, f32[3,3,256]{2,1,0:T(4,128)} %taps.1, f32[1,16]{1,0:T(1,128)} %bitcast.6, f32[33,64]{1,0:T(8,128)} %first.1, f32[1,64]{1,0:T(1,128)} %bitcast.7, f32[64,256]{1,0:T(8,128)} %fout.1, f32[1,256]{1,0:T(1,128)} %bitcast.5, ...), custom_call_target="tpu_custom_call" | custom-call | flops 3221225472 | bytes 12582912 | tf_op jit(solution)/shard_map/pallas_call | solution.py:536
  62.4 1.7 %copy.16 = bf16[512,256]{1,0:T(8,128)(2,1)} copy(bf16[512,256]{1,0:T(8,128)(2,1)} %shard_map.136) | data formatting | bytes 524288

commit v5 on v4

--- a/solution.py
+++ b/solution.py
@@ -249,9 +249,9 @@
 
 def operator_kernel(
     n_seq, n_ch,
-    tok_hbm, w_hbm, taps, band, first, bias, fout, decay, outer_hbm, twist_hbm, inner_hbm, inner_back_hbm, outer_back_hbm, wout_hbm,
+    tok_hbm, w_hbm, taps_hbm, band_hbm, first_hbm, bias_hbm, fout_hbm, decay_hbm, outer_hbm, twist_hbm, inner_hbm, inner_back_hbm, outer_back_hbm, wout_hbm,
     out_ref,
-    tok, w, outer, twist, inner, inner_back, outer_back,
+    tok, w, taps, band, first, bias, fout, decay, outer, twist, inner, inner_back, outer_back,
     tap_cols, fout_rows, decay_cols, padded, send4, pro_recv, gated_send, gated,
     grid32, x_all, a_all, rows_all, imp_spec, src_spec,
     load_sem, pro_ssem, pro_rsem, gat_ssem, gat_rsem, *out_scratch,
@@ -278,7 +278,13 @@
         pltpu.make_async_copy(inner_back_hbm, inner_back, load_sem.at[8]),
         pltpu.make_async_copy(outer_back_hbm, outer_back, load_sem.at[9]),
     ]
-    for copy in loads:
+    small = [
+        pltpu.make_async_copy(a, b, load_sem.at[10 + i])
+        for i, (a, b) in enumerate(
+            [(taps_hbm, taps), (fout_hbm, fout), (decay_hbm, decay), (band_hbm, band), (first_hbm, first), (bias_hbm, bias)]
+        )
+    ]
+    for copy in loads[:2] + small + loads[2:]:
         copy.start()
 
     barrier = pltpu.get_barrier_semaphore()
@@ -297,6 +303,8 @@
     for peer in (out.up, out.down):
         pl.semaphore_signal(barrier, inc=1, device_id=peer, device_id_type=MESH)
 
+    for copy in small:
+        copy.wait()
     for g in range(3):
         for i in range(3):
             tap_cols[g, i] = jnp.broadcast_to(taps[i, g : g + 1, :], (RADIX, slab)).T
@@ -515,6 +523,12 @@
     scratch = [
         pltpu.VMEM((rows, width), BF),
         pltpu.VMEM((3, width, slab), BF),
+        pltpu.VMEM(short_taps.shape, F32),
+        pltpu.VMEM((1, band_freq.shape[0]), F32),
+        pltpu.VMEM(filter_first.shape, F32),
+        pltpu.VMEM((1, filter_bias.shape[0]), F32),
+        pltpu.VMEM(filter_out.shape, F32),
+        pltpu.VMEM((1, slab), F32),
         *[pltpu.VMEM(t.shape, t.dtype) for t in tables],
         pltpu.VMEM((3, 3, slab, RADIX), F32),
         pltpu.VMEM((slab, filter_out.shape[0]), F32),
@@ -530,13 +544,13 @@
         pltpu.VMEM((channels * HALF, 2 * RADIX), BF),
         pltpu.VMEM((channels * HALF, 2 * RADIX), F32),
         pltpu.VMEM((channels * HALF, 2 * RADIX), F32),
-        dma((10,)), dma((3, n_seq)), dma((3, n_seq)), dma((2, 2, n_seq)), dma((2, 2, n_seq)),
+        dma((16,)), dma((3, n_seq)), dma((3, n_seq)), dma((2, 2, n_seq)), dma((2, 2, n_seq)),
         *spread_scratch(n_ch, rows, slab, out_weight.shape[1] // n_ch),
     ]
     return pl.pallas_call(
         functools.partial(operator_kernel, n_seq, n_ch),
-        out_shape=jax.ShapeDtypeStruct((rows, slab), BF),
-        in_specs=[anyspec] * 2 + [vspec] * 6 + [anyspec] * 6,
+        out_shape=pltpu.VMEM((rows, slab), BF),
+        in_specs=[anyspec] * 14,
         out_specs=vspec,
         scratch_shapes=scratch,
         compiler_params=pltpu.CompilerParams(collective_id=0, has_side_effects=True, vmem_limit_bytes=56 * 2**20),

time: 64.2 us -> 62 us (0.966)
  Pallas kernels: 62.3 us -> 61.2 us
  local copies, waits for them, and re-layouts: 1.67 us -> 0.71 us
    pallas_call x1, Pallas kernels: 62.3 us -> 61.2 us  [operator_rows(): pl.pallas_call(functools.partial(operator_kernel, n_seq, n_ch), out_shape...]
    unnamed x1, local copies, waits for them, and re-layouts: 1.67 us -> 0.71 us
where the time goes in v5:
time: 62 us
  Pallas kernels  61.2 us (99%)
  local copies, waits for them, and re-layouts  0.71 us (1%)
    pallas_call x1, Pallas kernels, operator_rows(): pl.pallas_call(functools.partial(operator_kernel, n_seq, n_ch), out_shape...  61.2 us

profile of v5, /device:TPU:1, one launch (start us, length us, event | category | flops | bytes accessed | tf_op | source)
XLA Modules:
  0.0 62.0 jit_solution(10124238834090773763)
XLA Ops:
  0.0 61.2 %shard_map.136 = bf16[512,256]{1,0:T(8,128)(2,1)S(1)} custom-call(bf16[512,4096]{1,0:T(8,128)(2,1)} %tok_hbm.1, bf16[3,4096,256]{2,1,0:T(8,128)(2,1)} %bitcast.4, f32[3,3,256]{2,1,0:T(4,128)} %taps_hbm.1, f32[1,16]{1,0:T(1,128)} %bitcast.6, f32[33,64]{1,0:T(8,128)} %first_hbm.1, f32[1,64]{1,0:T(1,128)} %bitcast.7, f32[64,256]{1,0:T(8,128)} %fout_hbm.1, ...), custom_call_target="tpu_custom_call" | custom-call | flops 3221225472 | bytes 12582912 | tf_op jit(solution)/shard_map/pallas_call | solution.py:550
  61.2 0.7 %copy.16 = bf16[512,256]{1,0:T(8,128)(2,1)} copy(bf16[512,256]{1,0:T(8,128)(2,1)S(1)} %shard_map.136) | data formatting | bytes 524288

commit v6 on v5

--- a/solution.py
+++ b/solution.py
@@ -481,8 +481,8 @@
     for part in (0, 1):
 
         def both_sides(p):
+            gated_copy(1, part, p).start()
             gated_copy(0, part, p).start()
-            gated_copy(1, part, p).start()
 
         each_peer(both_sides)
         gated_copy(1, part, me).start()
@@ -490,7 +490,7 @@
     out.pass_weights(range(3))
 
     def take_gated(part):
-        for side in (0, 1):
+        for side in (1, 0):
             each_peer(lambda p: gated_arrive(side, part, p).wait_recv())
             if side:
                 gated_arrive(1, part, me).wait_recv()

time: 62 us -> 62.2 us (level)
  no operation moved by 1% of the time
where the time goes in v6:
time: 62.2 us; the launch traced here: 62.1 us
  Pallas kernels  61.4 us (99%)
  local copies, waits for them, and re-layouts  0.71 us (1%)
    pallas_call x1, Pallas kernels, operator_rows(): pl.pallas_call(functools.partial(operator_kernel, n_seq, n_ch), out_shape...  61.4 us

profile of v6, /device:TPU:1, one launch (start us, length us, event | category | flops | bytes accessed | tf_op | source)
XLA Modules:
  0.0 62.1 jit_solution(7771659913922416125)
XLA Ops:
  0.0 61.4 %shard_map.136 = bf16[512,256]{1,0:T(8,128)(2,1)S(1)} custom-call(bf16[512,4096]{1,0:T(8,128)(2,1)} %tok_hbm.1, bf16[3,4096,256]{2,1,0:T(8,128)(2,1)} %bitcast.4, f32[3,3,256]{2,1,0:T(4,128)} %taps_hbm.1, f32[1,16]{1,0:T(1,128)} %bitcast.6, f32[33,64]{1,0:T(8,128)} %first_hbm.1, f32[1,64]{1,0:T(1,128)} %bitcast.7, f32[64,256]{1,0:T(8,128)} %fout_hbm.1, ...), custom_call_target="tpu_custom_call" | custom-call | flops 3221225472 | bytes 12582912 | tf_op jit(solution)/shard_map/pallas_call | solution.py:550
  61.4 0.7 %copy.16 = bf16[512,256]{1,0:T(8,128)(2,1)} copy(bf16[512,256]{1,0:T(8,128)(2,1)S(1)} %shard_map.136) | data formatting | bytes 524288
